TPU v7x, 512 devices: a whole 4x4x16 slice. The times are simulated.
512 devices in a mesh: team: 16 (over y_lo, x, core), row: 32 (over y_hi, z).
Axes of the slice: x: 4, y: 4 (y_hi: 2, y_lo: 2; y = y_hi * 2 + y_lo), z: 16, core: 2. Of those that a mesh axis runs over, the one named last changes fastest.
Arguments:
- features: bfloat16 [16384, 128], P('row'), may hold values from -6 to 6
- tile_vals: bfloat16 [32, 16, 128, 128, 128], P('row', 'team'), may hold values from 0 to 1
- tile_row: int32 [32, 16, 128], P('row', 'team'), may hold values from 0 to 3
- tile_col: int32 [32, 16, 128], P('row', 'team'), may hold values from 0 to 127, as said below
- tile_count: int32 [32, 16], P('row', 'team'), may hold values from 1 to 128, as said below
- weight: bfloat16 [128, 256], replicated, may hold values from -0.5 to 0.5
- bias: float32 [256], replicated, may hold values from -3 to 3
- cotangent: bfloat16 [16384, 256], P('row'), may hold values from -0.125 to 0.125
Outputs:
- activated: bfloat16 [16384, 256], P('row')
- weight_grad: float32 [128, 256], replicated
- bias_grad: float32 [256], replicated
Inputs may be any that keep to these rules, and one draw needn't show every extreme that they name: The owner index tile_col // 4 equals t + k * 16 for the device's team index t and some k < 2, in every slot. A device's live slots are its first tile_count slots; some device has all 128 live in every draw.
All inputs are finite; a program needn't handle non-finite values.
Results may differ from a plain program's by a relative error of at most 0.0075.
Values may be sent and summed in bfloat16 or wider, within the bound.
A program may use at most 64 MiB of HBM per device.

v0:
```python
import jax
import jax.numpy as jnp
from jax import lax
from jax.sharding import PartitionSpec as P

highest = lax.Precision.HIGHEST


def finish(aggregate, degree, grad_rows, weight, bias):
    normed = (aggregate / jnp.sqrt(degree)[:, None]).astype(jnp.bfloat16)
    pre_act = jnp.dot(normed, weight, preferred_element_type=jnp.float32) + bias
    activated = jax.nn.silu(pre_act).astype(jnp.bfloat16)
    gate_value = jax.nn.sigmoid(pre_act)
    delta = (
        grad_rows.astype(jnp.float32) * gate_value * (1.0 + pre_act * (1.0 - gate_value))
    ).astype(jnp.bfloat16)
    weight_grad = lax.dot_general(
        normed, delta, (((0,), (0,)), ((), ())), preferred_element_type=jnp.float32
    )
    bias_grad = jnp.sum(delta.astype(jnp.float32), axis=0)
    return (activated, weight_grad, bias_grad)


def per_device(features, tile_vals, tile_row, tile_col, tile_count, weight, bias, cotangent):
    local_rows, in_width = features.shape
    tile_side = tile_vals.shape[-1]
    local_blocks = local_rows // tile_side
    slot_total = tile_vals.shape[2]
    adjacency = tile_vals.reshape(slot_total, tile_side, tile_side)
    row_slot = tile_row.reshape(slot_total)
    col_slot = tile_col.reshape(slot_total)
    live_count = tile_count.reshape(())
    whole_rows = lax.all_gather(features, "row", axis=0, tiled=True)
    feature_table = whole_rows.reshape(-1, tile_side, in_width)
    slot_ids = jnp.arange(slot_total, dtype=jnp.int32)
    selector = (row_slot[:, None] == jnp.arange(local_blocks, dtype=jnp.int32)[None, :]) & (
        slot_ids < live_count
    )[:, None]
    selector = selector.astype(jnp.float32)
    products = jnp.einsum(
        "sij,sjf->sif", adjacency, feature_table[col_slot], preferred_element_type=jnp.float32
    )
    part_sum = jnp.einsum("sb,sif->bif", selector, products, precision=highest)
    row_sums = jnp.sum(adjacency, axis=2, dtype=jnp.float32)
    part_degree = jnp.einsum("sb,si->bi", selector, row_sums, precision=highest)
    aggregate = part_sum
    degree = part_degree
    aggregate = aggregate.reshape(local_rows, in_width)
    degree = degree.reshape(local_rows)
    aggregate, degree = lax.psum((aggregate, degree), "team")
    degree = degree + 1.0
    activated, weight_grad, bias_grad = finish(aggregate, degree, cotangent, weight, bias)
    weight_grad, bias_grad = lax.psum((weight_grad, bias_grad), "row")
    return (activated, weight_grad, bias_grad)


def solution(mesh):
    in_specs = (
        P("row", None),
        P("row", "team", None, None, None),
        P("row", "team", None),
        P("row", "team", None),
        P("row", "team"),
        P(),
        P(),
        P("row", None),
    )
    out_specs = (P("row", None), P(), P())
    return jax.shard_map(
        per_device, mesh=mesh, in_specs=in_specs, out_specs=out_specs, check_vma=False
    )
```

profile of v0, /device:TPU:24, one launch (start us, length us, event | category | flops | bytes accessed | tf_op | source)
XLA Modules:
  0.0 623.4 jit_solution(8110107016385595926)
XLA Ops:
  7.2 0.0 copy-start
  7.2 0.0 all-gather.2.cloned.1.call-start
  7.2 0.7 all-gather.2.cloned.1.call-update
  7.9 0.0 all-reduce.3.cloned.1.call-start
  8.6 0.7 fusion.12
  9.3 3.4 convert_reduce_fusion
  12.6 165.2 %all-gather.2.cloned.1.call-done = bf16[16384,128]{1,0:T(8,128)(2,1)} async-done(((bf16[512,128]{1,0:T(8,128)(2,1)}), bf16[16384,128]{1,0:T(8,128)(2,1)}) %all-gather.2.cloned.1.call-update) | async-done | bytes 4194320 | tf_op jit(solution)/shard_map/all_gather | solution.py:33
  177.9 5.2 gather_fusion
  183.1 9.8 %fusion.2 = f32[128,128,128]{2,1,0:T(8,128)} fusion(bf16[128,128,128]{2,1,0:T(8,128)(2,1)} %gather_fusion, bf16[1,1,128,128,128]{4,3,2,1,0:T(8,128)(2,1)} %param.9), kind=kOutput, calls=%fused_computation.4 | convolution fusion | flops 536870912 | bytes 16777216 | tf_op jit(solution)/shard_map/sij,sjf->sif/dot_general | solution.py:40
  192.9 9.3 %copy.12 = f32[128,128,128]{1,0,2:T(8,128)} copy(f32[128,128,128]{2,1,0:T(8,128)} %fusion.2) | data formatting | bytes 16777216 | tf_op jit(solution)/shard_map/sij,sjf->sif/dot_general | solution.py:40
  202.1 0.0 copy-done.1
  202.2 6.2 fusion
  208.4 0.7 copy.11
  209.1 0.0 all-reduce.3.cloned.1.call-update
  209.1 0.0 all-reduce.5.cloned.1.call-start
  209.2 0.1 convolution_bitcast_fusion
  209.3 27.1 %psum.29 = f32[512]{0:T(512)S(1)} all-reduce(f32[512]{0:T(512)S(1)} %convolution_bitcast_fusion), channel_id=1, replica_groups=mesh['team'=16,'row'=32] {'team'}, use_global_device_ids=true, to_apply=%region_2.0 | all-reduce | flops 512 | bytes 4096 | tf_op jit(solution)/shard_map/psum | solution.py:50
  236.5 100.6 %all-reduce.3.cloned.1.call-done = f32[512,128]{1,0:T(8,128)} async-done(((f32[512,128]{1,0:T(8,128)}), f32[512,128]{1,0:T(8,128)}) %all-reduce.3.cloned.1.call-update) | async-done | bytes 262160 | tf_op jit(solution)/shard_map/psum | solution.py:50
  337.1 2.2 convert_reduce_fusion.1
  339.3 1.0 fusion.13
  340.3 0.0 all-reduce.5.cloned.1.call-update
  340.3 77.4 %psum.31 = f32[256]{0:T(256)} all-reduce(f32[256]{0:T(256)S(1)} %get-tuple-element.3), channel_id=1, replica_groups=mesh['team'=16,'row'=32] {'row'}, use_global_device_ids=true, to_apply=%region_5.6 | all-reduce | flops 256 | bytes 2048 | tf_op jit(solution)/shard_map/psum | solution.py:53
  417.7 197.6 %all-reduce.5.cloned.1.call-done = f32[128,256]{1,0:T(8,128)} async-done(((f32[128,256]{1,0:T(8,128)}), f32[128,256]{1,0:T(8,128)}) %all-reduce.5.cloned.1.call-update) | async-done | bytes 131088 | tf_op jit(solution)/shard_map/psum | solution.py:53
  615.3 1.6 copy.16
  (11 shorter events, 0.0 us)
Async XLA Ops:
  7.2 329.9 %copy-start = (bf16[128,256]{1,0:T(8,128)(2,1)S(1)}, bf16[128,256]{1,0:T(8,128)(2,1)}, u32[]{:S(2)}) copy-start(bf16[128,256]{1,0:T(8,128)(2,1)} %param.13) | copy-start | bytes 196612
  7.2 170.7 %all-gather.2.cloned.1.call-start = ((), (), s32[]{:S(2)}) async-start(), calls=%async_computation | async-start | bytes 4325376 | tf_op jit(solution)/shard_map/all_gather | solution.py:33
  7.9 329.2 %all-reduce.3.cloned.1.call-start = ((), (), s32[]{:S(2)}) async-start(), calls=%async_computation.1 | async-start | bytes 524288 | tf_op jit(solution)/shard_map/psum | solution.py:50
  192.9 9.3 %copy-start.1 = (s32[1,1,128]{2,1,0:T(1,128)S(1)}, s32[1,1,128]{2,1,0:T(1,128)}, u32[]{:S(2)}) copy-start(s32[1,1,128]{2,1,0:T(1,128)} %param.10) | copy-start | bytes 1540
  202.1 134.9 %copy-start.2 = (bf16[512,256]{1,0:T(8,128)(2,1)S(1)}, bf16[512,256]{1,0:T(8,128)(2,1)}, u32[]{:S(2)}) copy-start(bf16[512,256]{1,0:T(8,128)(2,1)} %param.15) | copy-start | bytes 786436
  202.2 134.9 %copy-start.4 = (f32[256]{0:T(256)S(1)}, f32[256]{0:T(256)}, u32[]{:S(2)}) copy-start(f32[256]{0:T(256)} %param.14) | copy-start | bytes 3076
  209.1 406.2 %all-reduce.5.cloned.1.call-start = ((), (), s32[]{:S(2)}) async-start(), calls=%async_computation.2 | async-start | bytes 262144 | tf_op jit(solution)/shard_map/psum | solution.py:53
  337.1 2.2 copy-start.3
Sparse Core Ops, SparseCore 0:
  11.1 166.6 all-gather.1
  209.2 127.7 all-reduce.2
  340.8 274.4 all-reduce.4
where the time goes:
time: 624 us; the launch traced here: 623 us
  waiting for transfers between devices  464 us (74%)
  blocking collectives  105 us (17%)
  matrix products  19.3 us (3%)
  local copies, waits for them, and re-layouts  16.8 us (3%)
  between operations  14.4 us (2%)
    psum x1, waiting for transfers between devices, per_device(): weight_grad, bias_grad = lax.psum((weight_grad, bias_grad), 'row')  198 us
    all_gather x1, waiting for transfers between devices, per_device(): whole_rows = lax.all_gather(features, 'row', axis=0, tiled=True)  165 us
    psum x1, waiting for transfers between devices, per_device(): aggregate, degree = lax.psum((aggregate, degree), 'team')  101 us
    psum x1, blocking collectives, per_device(): weight_grad, bias_grad = lax.psum((weight_grad, bias_grad), 'row')  77.4 us
    psum x1, blocking collectives, per_device(): aggregate, degree = lax.psum((aggregate, degree), 'team')  27.1 us
  transfers between devices with their start and end apart: 3, of which 3 were waited for; matrix products, arithmetic and copies ran while one was open for 1% of the time, Pallas kernels for 0%

commit v1 on v0

v1 whole, which is shorter than its diff:
```python
import functools

import jax
import jax.numpy as jnp
from jax import lax
from jax.experimental import pallas as pl
from jax.experimental.pallas import tpu as pltpu
from jax.sharding import PartitionSpec as P

MESH = pl.DeviceIdType.MESH
BF16, F32 = jnp.bfloat16, jnp.float32
SIDE = 128
GROUP = 8


def wait_bytes(ref, sem):
    pltpu.make_async_copy(ref, ref, sem).wait()


def kernel(
    T, Z, feat, tiles, trow, tcol, tcount, weight, bias, cot,
    act_out, dw_out, db_out,
    a_vm, zbuf, table, agg, aggs, deg, degs, dgacc, degr, aggr, nbuf, w_vm, b_vm, c_vm, act_vm,
    delta, dwp, piece, pieces_in, full, dw_all,
    tile_sem, w_sem, b_sem, c_sem, a1_send, a1_recv, a2_send, a2_recv, g_send, g_recv, p_send, p_recv,
    n_send, n_recv, d1_send, d1_recv, d2_send, d2_recv, e_send, e_recv, act_sem,
):
    R = 2 * Z
    slots = a_vm.shape[0]
    rows = nbuf.shape[0]
    blocks = rows // SIDE
    PR = rows // T
    r, t = lax.axis_index("row"), lax.axis_index("team")
    k, z = r // Z, r % Z

    def remote(src, dst, ssem, rsem, row, team):
        pltpu.make_async_remote_copy(
            src_ref=src, dst_ref=dst, send_sem=ssem, recv_sem=rsem,
            device_id={"row": row, "team": team}, device_id_type=MESH,
        ).start()

    tile_copy = pltpu.make_async_copy(tiles, a_vm, tile_sem)
    tile_copy.start()
    mine = pl.ds(pl.multiple_of(t * PR, PR), PR)
    pltpu.make_async_copy(feat.at[mine], zbuf.at[z], a1_recv.at[z]).start()
    w_copy = pltpu.make_async_copy(weight, w_vm, w_sem)
    b_copy = pltpu.make_async_copy(bias, b_vm, b_sem)
    c_copy = pltpu.make_async_copy(cot, c_vm, c_sem)
    w_copy.start()
    b_copy.start()
    c_copy.start()

    barrier = pltpu.get_barrier_semaphore()

    @pl.loop(1, R)
    def _(o):
        pl.semaphore_signal(barrier, inc=1, device_id={"row": (r + o) % R, "team": t}, device_id_type=MESH)

    @pl.loop(1, T)
    def _(o):
        u = (t + o) % T
        pl.semaphore_signal(barrier, inc=1, device_id={"row": z, "team": u}, device_id_type=MESH)
        pl.semaphore_signal(barrier, inc=1, device_id={"row": Z + z, "team": u}, device_id_type=MESH)

    pl.semaphore_wait(barrier, R - 1 + 2 * (T - 1))

    def far_first(i):
        d = Z // 2 - (i + 1) // 2
        return jnp.where(i % 2 == 0, d, Z - d)

    @pl.loop(0, Z - 1)
    def _(i):
        to = (z + far_first(i)) % Z
        remote(feat.at[mine], zbuf.at[z], a1_send, a1_recv.at[z], k * Z + to, t)

    table[2 * blocks] = jnp.zeros((SIDE, SIDE), BF16)
    dgacc[...] = jnp.zeros_like(dgacc)
    lane = lax.broadcasted_iota(jnp.int32, (SIDE, SIDE), 1)
    lane_block = lane // (SIDE // blocks)
    count = tcount[0, 0]
    tile_copy.wait()

    @pl.loop(0, slots // GROUP)
    def _(c):
        left = jnp.concatenate([a_vm[c * GROUP + g] for g in range(GROUP)], axis=1)
        right = []
        for g in range(GROUP):
            s = c * GROUP + g
            b = jnp.where(s < count, trow[s], blocks)
            right.append(jnp.where(lane_block == b, 1.0, 0.0).astype(BF16))
        dgacc[...] += jnp.dot(left, jnp.concatenate(right, axis=0), preferred_element_type=F32)

    for b in range(blocks):
        col = jnp.sum(jnp.where(lane_block == b, dgacc[...], 0.0), axis=1, keepdims=True) * (blocks / SIDE)
        col = jnp.broadcast_to(col, (SIDE, SIDE))
        high = col.astype(BF16).astype(F32)
        deg[pl.ds(b * SIDE, SIDE), :] = col
        degs[pl.ds(b * SIDE, SIDE), :] = jnp.where(lane < SIDE // 2, high, col - high).astype(BF16)

    @pl.loop(1, T)
    def _(o):
        u = (t + o) % T
        part = pl.ds(pl.multiple_of(u * PR, PR), PR)
        remote(degs.at[part], degr.at[o - 1], g_send, g_recv, r, u)

    spot = (k * T + t) * PR
    place = (spot // SIDE, pl.ds(pl.multiple_of(spot % SIDE, PR), PR))

    def forward(source):
        wait_bytes(zbuf.at[source], a1_recv.at[source])
        remote(zbuf.at[source], table.at[place], a2_send, a2_recv, (1 - k) * Z + z, source)

        @pl.when(source != t)
        def _():
            remote(zbuf.at[source], table.at[place], a2_send, a2_recv, k * Z + z, source)

    forward(z)

    @pl.loop(0, Z - 1)
    def _(i):
        forward((z - far_first(i) + Z) % Z)

    table[place] = zbuf[t]
    wait_bytes(agg.at[pl.ds(0, (2 * T - 1) * PR // 2)], a2_recv)

    pair = 2 * SIDE
    owner_bits = (blocks * T).bit_length() - 1
    for half in range(blocks // 2):
        for j in range(2):
            agg[pl.ds((2 * half + j) * SIDE, SIDE), :] = jnp.zeros((SIDE, SIDE), F32)

        @pl.loop(0, slots // GROUP)
        def _(c):
            left = jnp.concatenate([a_vm[c * GROUP + g] for g in range(GROUP)], axis=1)
            right = []
            for g in range(GROUP):
                s = c * GROUP + g
                col = tcol[s]
                at = (col >> owner_bits) * blocks + (col & (blocks - 1))
                b = jnp.where(s < count, trow[s], blocks)
                ends = []
                for j in range(2):
                    index = jnp.where(b == 2 * half + j, at, 2 * blocks)
                    ends.append(table[index])
                right.append(jnp.concatenate(ends, axis=1))
            got = jnp.dot(left, jnp.concatenate(right, axis=0), preferred_element_type=F32)
            for j in range(2):
                agg[pl.ds((2 * half + j) * SIDE, SIDE), :] += got[:, j * SIDE:(j + 1) * SIDE]

        span = pl.ds(half * pair, pair)
        aggs[span, :] = agg[span, :].astype(BF16)
        owners = pair // PR

        @pl.loop(half * owners, (half + 1) * owners)
        def _(u):
            @pl.when(u != t)
            def _():
                part = pl.ds(pl.multiple_of(u * PR, PR), PR)
                remote(aggs.at[part], aggr.at[(u - t + T) % T - 1], p_send, p_recv, r, u)

    wait_bytes(degr, g_recv)
    degree = jnp.sum(degr[0].astype(F32), axis=1, keepdims=True)
    for o in range(1, T - 1):
        degree += jnp.sum(degr[o].astype(F32), axis=1, keepdims=True)
    degree = degree * (2.0 / SIDE) + deg[mine, :] + 1.0
    root = jnp.sqrt(degree)
    wait_bytes(aggr, p_recv)
    total = agg[mine, :]
    for o in range(T - 1):
        total += aggr[o].astype(F32)
    nbuf[mine, :] = (total / root).astype(BF16)

    @pl.loop(1, T)
    def _(o):
        remote(nbuf.at[mine], nbuf.at[mine], n_send, n_recv, r, (t + o) % T)

    w_copy.wait()
    b_copy.wait()
    c_copy.wait()
    wait_bytes(nbuf.at[pl.ds(0, (T - 1) * PR)], n_recv)

    db = None
    for b in range(blocks):
        span = pl.ds(b * SIDE, SIDE)
        pre = jnp.dot(nbuf[span, :], w_vm[...], preferred_element_type=F32) + b_vm[...]
        gate = 1.0 / (1.0 + jnp.exp(-pre))
        act_vm[span, :] = (pre * gate).astype(BF16)
        d = (c_vm[span, :].astype(F32) * gate * (1.0 + pre * (1.0 - gate))).astype(BF16)
        delta[span, :] = d
        part = jnp.sum(d.astype(F32), axis=0, keepdims=True)
        db = part if db is None else db + part
    act_copy = pltpu.make_async_copy(act_vm, act_out, act_sem)
    act_copy.start()
    dwp[...] = lax.dot_general(nbuf[...], delta[...], (((0,), (0,)), ((), ())), preferred_element_type=F32)

    SR = SIDE // T
    n = 2 * SR // Z
    own = dwp[pl.ds(pl.multiple_of(t * SR, SR), SR), :]
    for q in range(Z):
        for h in range(n):
            j = q * n + h
            piece[q, :, h * SIDE:(h + 1) * SIDE] = own[j // 2:j // 2 + 1, (j % 2) * SIDE:(j % 2 + 1) * SIDE]
        piece[q, :, n * SIDE:] = db[:, (q % 2) * SIDE:(q % 2 + 1) * SIDE]

    @pl.loop(1, R)
    def _(o):
        to = (r + o) % R
        remote(piece.at[to % Z], pieces_in.at[o - 1], d1_send, d1_recv, to, t)

    wait_bytes(pieces_in, d1_recv)
    full[z] = piece[z] + jnp.sum(pieces_in[...], axis=0)

    @pl.loop(1, Z)
    def _(o):
        remote(full.at[z], full.at[z], d2_send, d2_recv, k * Z + (z + o) % Z, t)

    wait_bytes(full.at[pl.ds(0, Z - 1)], d2_recv)
    slice_rows = pl.ds(pl.multiple_of(t * SR, SR), SR)
    lines = []
    for i in range(SR):
        halves = [full[j // n, :, (j % n) * SIDE:(j % n + 1) * SIDE] for j in (2 * i, 2 * i + 1)]
        lines.append(jnp.concatenate(halves, axis=1))
    dw_all[slice_rows, :] = jnp.concatenate(lines, axis=0)

    @pl.loop(1, T)
    def _(o):
        remote(dw_all.at[slice_rows], dw_all.at[slice_rows], e_send, e_recv, r, (t + o) % T)

    for h in range(2):
        db_out[:, h * SIDE:(h + 1) * SIDE] = full[h, :, n * SIDE:]

    wait_bytes(zbuf.at[pl.ds(0, Z - 1)], a1_send)
    wait_bytes(agg.at[pl.ds(0, (2 * T - 1) * PR // 2)], a2_send)
    wait_bytes(degr, g_send)
    wait_bytes(aggr, p_send)
    wait_bytes(nbuf.at[pl.ds(0, (T - 1) * PR)], n_send)
    wait_bytes(pieces_in, d1_send)
    wait_bytes(full.at[pl.ds(0, Z - 1)], d2_send)
    act_copy.wait()
    rest = dw_all.at[pl.ds(0, (T - 1) * SR)]
    wait_bytes(rest, e_send)
    wait_bytes(rest, e_recv)
    dw_out[...] = dw_all[...]


def per_device(T, Z, features, tile_vals, tile_row, tile_col, tile_count, weight, bias, cotangent):
    rows, width = features.shape
    slots = tile_vals.shape[2]
    hidden = weight.shape[1]
    PR = rows // T
    SR = SIDE // T
    n = 2 * SR // Z
    wide = (n + 1) * SIDE
    any_spec = pl.BlockSpec(memory_space=pl.ANY)
    hbm = pl.BlockSpec(memory_space=pltpu.HBM)
    smem = pl.BlockSpec(memory_space=pltpu.SMEM)
    vmem = pl.BlockSpec(memory_space=pltpu.VMEM)
    dma = pltpu.SemaphoreType.DMA
    V = pltpu.VMEM
    activated, dw, db = pl.pallas_call(
        functools.partial(kernel, T, Z),
        out_shape=(
            jax.ShapeDtypeStruct((rows, hidden), BF16),
            jax.ShapeDtypeStruct((width, hidden), F32),
            jax.ShapeDtypeStruct((1, hidden), F32),
        ),
        in_specs=[hbm, hbm, smem, smem, smem, hbm, hbm, hbm],
        out_specs=(any_spec, vmem, vmem),
        scratch_shapes=[
            V((slots, SIDE, SIDE), BF16),
            V((Z, PR, width), BF16),
            V((2 * rows // SIDE + 1, SIDE, width), BF16),
            V((rows, width), F32),
            V((rows, width), BF16),
            V((rows, SIDE), F32),
            V((rows, SIDE), BF16),
            V((SIDE, SIDE), F32),
            V((T - 1, PR, SIDE), BF16),
            V((T - 1, PR, width), BF16),
            V((rows, width), BF16),
            V((width, hidden), BF16),
            V((1, hidden), F32),
            V((rows, hidden), BF16),
            V((rows, hidden), BF16),
            V((rows, hidden), BF16),
            V((width, hidden), F32),
            V((Z, 1, wide), F32),
            V((2 * Z - 1, 1, wide), F32),
            V((Z, 1, wide), F32),
            V((width, hidden), F32),
            dma, dma, dma, dma,
            dma, dma((Z,)),
            dma, dma, dma, dma, dma, dma, dma, dma, dma, dma, dma, dma, dma, dma, dma,
        ],
        compiler_params=pltpu.CompilerParams(
            collective_id=0, has_side_effects=True, vmem_limit_bytes=56 * 1024 * 1024
        ),
        cost_estimate=pl.CostEstimate(
            flops=2 * slots * SIDE * SIDE * width, bytes_accessed=2 * slots * SIDE * SIDE, transcendentals=rows * hidden
        ),
    )(
        features,
        tile_vals.reshape(slots, SIDE, SIDE),
        tile_row.reshape(slots),
        tile_col.reshape(slots),
        tile_count,
        weight,
        bias.reshape(1, hidden),
        cotangent,
    )
    return activated, dw, db.reshape(hidden)


def solution(mesh):
    in_specs = (
        P("row", None),
        P("row", "team", None, None, None),
        P("row", "team", None),
        P("row", "team", None),
        P("row", "team"),
        P(),
        P(),
        P("row", None),
    )
    out_specs = (P("row", None), P(), P())
    T = mesh.shape["team"]
    Z = mesh.shape["row"] // 2
    return jax.shard_map(
        functools.partial(per_device, T, Z), mesh=mesh, in_specs=in_specs, out_specs=out_specs, check_vma=False
    )
```

time: 624 us -> 76.3 us (0.12)
  the two profiles are of different devices: /device:TPU:24 before, /device:TPU:1 now
where the time goes in v1:
time: 76.3 us; the launch traced here: 76.1 us
  Pallas kernels  70.4 us (92%)
  local copies, waits for them, and re-layouts  4.43 us (6%)
  between operations  1.29 us (2%)
    pallas_call x1, Pallas kernels, per_device(): pl.pallas_call(functools.partial(kernel, T, Z), out_shape=(jax.ShapeDtype...  70.4 us
    unnamed x3, local copies, waits for them, and re-layouts  4.43 us

profile of v1, /device:TPU:1, one launch (start us, length us, event | category | flops | bytes accessed | tf_op | source)
XLA Modules:
  0.0 76.1 jit_solution(17634615692639498327)
XLA Ops:
  1.3 70.4 %shard_map.103 = (bf16[512,256]{1,0:T(8,128)(2,1)}, f32[128,256]{1,0:T(8,128)}, f32[1,256]{1,0:T(1,128)}) custom-call(bf16[512,128]{1,0:T(8,128)(2,1)} %feat.1, bf16[128,128,128]{2,1,0:T(8,128)(2,1)} %bitcast.5, s32[128]{0:T(128)} %bitcast.8, s32[128]{0:T(128)} %bitcast.9, s32[1,1]{1,0:T(1,128)S(6)} %copy.14.tcount, bf16[128,256]{1,0:T(8,128)(2,1)} %weight.1, ...), custom_call_target="tpu_custom_call" | custom-call | flops 536870912 | bytes 4194304 | tf_op jit(solution)/shard_map/pallas_call | solution.py:260
  71.7 1.7 %copy.15 = bf16[512,256]{1,0:T(8,128)(2,1)} copy(bf16[512,256]{1,0:T(8,128)(2,1)} %get-tuple-element.12) | data formatting | bytes 524288
  73.4 1.6 %copy.16 = f32[128,256]{1,0:T(8,128)} copy(f32[128,256]{1,0:T(8,128)} %get-tuple-element.13) | data formatting | bytes 262144
  74.9 1.2 %copy.17 = f32[256]{0:T(256)} copy(f32[256]{0:T(256)} %bitcast.7) | data formatting | bytes 2048

commit v2 on v0

v2 whole, which is shorter than its diff:
```python
import functools

import jax
import jax.numpy as jnp
from jax import lax
from jax.experimental import pallas as pl
from jax.experimental.pallas import tpu as pltpu
from jax.sharding import PartitionSpec as P

MESH = pl.DeviceIdType.MESH
BF16, F32 = jnp.bfloat16, jnp.float32
SIDE = 128


def wait_bytes(ref, sem):
    pltpu.make_async_copy(ref, ref, sem).wait()


def each(count, body, first=0):
    unroll = 5

    @pl.loop(0, count // unroll)
    def _(i):
        for j in range(unroll):
            body(first + i * unroll + j)

    for j in range(count - count % unroll, count):
        body(first + j)


def kernel(
    T, Z, feat, tiles, trow, tcol, tcount, weight, bias, cot,
    act_out, dw_out, db_out,
    a_vm, up, dn, table, high, low, running, order_v, order, row_v, col_v, count_s,
    agg, aggs, deg, degs, degr, aggr, nbuf, w_vm, b_vm, c_vm,
    piece, piece_in, lined, final,
    tile_sem, row_sem, col_sem, count_sem, order_sem, w_sem, b_sem, c_sem,
    up_send, up_recv, dn_send, dn_recv, a2_send, a2_recv, g_send, g_recv, p_send, p_recv,
    n_send, n_recv, x_send, x_recv, d_send, d_recv, e_send, e_recv,
):
    R = 2 * Z
    slots = a_vm.shape[0]
    rows = nbuf.shape[0]
    blocks = rows // SIDE
    wide = 2 * blocks
    PR = rows // T
    rem = lax.rem
    r, t = lax.axis_index("row"), lax.axis_index("team")
    k, z = lax.div(r, Z), rem(r, Z)

    def remote(src, dst, ssem, rsem, row, team):
        pltpu.make_async_remote_copy(
            src_ref=src, dst_ref=dst, send_sem=ssem, recv_sem=rsem,
            device_id={"row": row, "team": team}, device_id_type=MESH,
        ).start()

    barrier = pltpu.get_barrier_semaphore()
    S = Z // 4
    near = [*range(1, S + 1), *range(Z - S, Z)]

    def signal(row, team):
        pl.semaphore_signal(barrier, inc=1, device_id={"row": row, "team": team}, device_id_type=MESH)

    def in_plane(body):
        def both(o):
            u = rem(t + o, T)
            body(0, u)
            body(1, u)

        body(1 - k, t)
        each(T - 1, both, 1)

    for o in near:
        signal(k * Z + rem(z + o, Z), t)
    in_plane(lambda kk, u: signal(kk * Z + z, u))

    row_copy = pltpu.make_async_copy(trow, row_v, row_sem)
    col_copy = pltpu.make_async_copy(tcol, col_v, col_sem)
    count_copy = pltpu.make_async_copy(tcount, count_s, count_sem)
    row_copy.start()
    col_copy.start()
    count_copy.start()
    mine = pl.ds(pl.multiple_of(t * PR, PR), PR)
    tile_copy = pltpu.make_async_copy(tiles, a_vm, tile_sem)
    tile_copy.start()
    w_copy = pltpu.make_async_copy(weight, w_vm, w_sem)
    b_copy = pltpu.make_async_copy(bias, b_vm, b_sem)
    c_copy = pltpu.make_async_copy(cot, c_vm, c_sem)
    w_copy.start()
    b_copy.start()
    c_copy.start()

    pl.semaphore_wait(barrier, len(near) + 2 * T - 1)

    ways = ((up, up_send, up_recv, 1, Z // 2), (dn, dn_send, dn_recv, -1, Z // 2 - 1))
    own_piece = feat.at[mine]
    for d in range(S, 0, -1):
        for buf, ssem, rsem, sign, far in ways:
            remote(own_piece, buf.at[d], ssem, rsem.at[d], k * Z + rem(z + sign * d + Z, Z), t)

    place = pl.ds(pl.multiple_of((k * T + t) * PR, PR), PR)

    def forward(piece_ref, source):
        remote(piece_ref, table.at[place], a2_send, a2_recv, (1 - k) * Z + z, source)

        @pl.when(source != t)
        def _():
            remote(piece_ref, table.at[place], a2_send, a2_recv, k * Z + z, source)

        @pl.when(source == t)
        def _():
            pltpu.make_async_copy(piece_ref, table.at[place], a2_recv).start()

    def relay():
        for buf, ssem, rsem, sign, far in ways:
            wait_bytes(buf.at[S], rsem.at[S])
            for e in range(far - S, 0, -1):
                remote(buf.at[S], buf.at[S + e], ssem, rsem.at[S + e], k * Z + rem(z + sign * e + Z, Z), t)

    def pass_on(distances):
        for d in distances:
            for buf, ssem, rsem, sign, far in ways:
                if d <= far:
                    if d != S:
                        wait_bytes(buf.at[d], rsem.at[d])
                    forward(buf.at[d], rem(z - sign * d + Z, Z))

    forward(own_piece, z)

    row_copy.wait()
    col_copy.wait()
    count_copy.wait()
    lane = lax.broadcasted_iota(jnp.int32, (slots, SIDE), 1)
    line = lax.broadcasted_iota(jnp.int32, (slots, SIDE), 0)
    owner_bits = (blocks * T).bit_length() - 1
    col = col_v[...]
    key = row_v[...] * wide + (col >> owner_bits) * blocks + (col & (blocks - 1))
    ids = lax.broadcasted_iota(jnp.int32, (1, slots), 1)
    key = jnp.where(ids < count_s[0, 0], key, SIDE - 1)
    key = jnp.broadcast_to(key, (slots, slots))
    slot = lax.broadcasted_iota(jnp.int32, (slots, slots), 1)
    here = lax.broadcasted_iota(jnp.int32, (slots, slots), 0)
    down = jnp.sum(jnp.where(slot == here, key, 0), axis=1, keepdims=True)
    ahead = (key < down) | ((key == down) & (slot < here))
    rank = jnp.sum(jnp.where(ahead, 1, 0), axis=1, keepdims=True)

    def across(mask, what):
        return jnp.sum(jnp.where(mask, what, 0), axis=0, keepdims=True)

    order_v[0:1, :] = across(rank == lane, line)
    key_at = across(rank == lane, down)
    key_before = across(rank + 1 == lane, down)
    order_v[1:2, :] = jnp.where((key_at == key_before) & (lane[0:1] > 0), 1, 0)
    population = across(down == lane, 1)
    order_v[2:3, :] = jnp.where(population > 0, across(down <= lane, 1) - 1, slots)
    order_copy = pltpu.make_async_copy(order_v, order, order_sem)
    order_copy.start()
    high[slots] = jnp.zeros((SIDE, SIDE), BF16)
    low[slots] = jnp.zeros((SIDE, SIDE), BF16)
    running[...] = jnp.zeros_like(running)
    relay()
    pass_on(range(S, 0, -1))
    order_copy.wait()
    tile_copy.wait()

    chunk = 8

    def sum_tiles(c):
        held = running[...]
        for g in range(chunk):
            i = c * chunk + g
            held = jnp.where(order[1, i] > 0, held, 0.0) + a_vm[order[0, i]].astype(F32)
            top = held.astype(BF16)
            high[i] = top
            low[i] = (held - top.astype(F32)).astype(BF16)
        running[...] = held

    chunks = slots // chunk
    pl.loop(0, chunks // 2)(sum_tiles)
    pass_on(range(Z // 2, S, -1))
    pl.loop(chunks // 2, chunks)(sum_tiles)

    def dense(part, half):
        bands = []
        for b in (2 * half, 2 * half + 1):
            bands.append(jnp.concatenate([part[order[2, b * wide + c]] for c in range(wide)], axis=1))
        return jnp.concatenate(bands, axis=0)

    def product(half, right):
        got = jnp.dot(dense(high, half), right, preferred_element_type=F32)
        return got + jnp.dot(dense(low, half), right, preferred_element_type=F32)

    pair = 2 * SIDE
    left_lanes = lax.broadcasted_iota(jnp.int32, (pair, SIDE), 1) < SIDE // 2
    for half in range(blocks // 2):
        span = pl.ds(half * pair, pair)
        sums = product(half, jnp.ones((wide * SIDE, SIDE), BF16))
        top = sums.astype(BF16).astype(F32)
        deg[span, :] = sums
        degs[span, :] = jnp.where(left_lanes, top, sums - top).astype(BF16)

    def give_degree(o):
        u = rem(t + o, T)
        part = pl.ds(pl.multiple_of(u * PR, PR), PR)
        remote(degs.at[part], degr.at[o - 1], g_send, g_recv, r, u)

    each(T - 1, give_degree, 1)
    wait_bytes(table, a2_recv)

    owners = pair // PR
    for half in range(blocks // 2):
        span = pl.ds(half * pair, pair)
        got = product(half, table[...])
        agg[span, :] = got
        aggs[span, :] = got.astype(BF16)

        def give_part(u):
            @pl.when(u != t)
            def _():
                part = pl.ds(pl.multiple_of(u * PR, PR), PR)
                remote(aggs.at[part], aggr.at[rem(u - t + T, T) - 1], p_send, p_recv, r, u)

        each(owners, give_part, half * owners)

    wait_bytes(degr, g_recv)
    degree = degr[0].astype(F32)
    for o in range(1, T - 1):
        degree += degr[o].astype(F32)
    degree = jnp.sum(degree, axis=1, keepdims=True) * (2.0 / SIDE) + deg[mine, :] + 1.0
    root = jnp.sqrt(degree)
    wait_bytes(aggr, p_recv)
    total = agg[mine, :]
    for o in range(T - 1):
        total += aggr[o].astype(F32)
    w_copy.wait()
    b_copy.wait()
    c_copy.wait()

    def layer(normed):
        pre = jnp.dot(normed, w_vm[...], preferred_element_type=F32) + b_vm[...]
        return pre, 1.0 / (1.0 + jnp.exp(-pre))

    normed = (total / root).astype(BF16)
    nbuf[mine, :] = normed
    pre, gate = layer(normed)
    delta = (c_vm[mine, :].astype(F32) * gate * (1.0 + pre * (1.0 - gate))).astype(BF16)
    db = jnp.sum(delta.astype(F32), axis=0, keepdims=True)
    dw = lax.dot_general(normed, delta, (((0,), (0,)), ((), ())), preferred_element_type=F32)

    SR = SIDE // T
    HR = SR // 2
    n = 2 * HR
    for q in range(2):
        for u in range(T):
            for j in range(n):
                i = u * SR + q * HR + j // 2
                piece[q * T + u, :, j * SIDE:(j + 1) * SIDE] = dw[i:i + 1, (j % 2) * SIDE:(j % 2 + 1) * SIDE]
            piece[q * T + u, :, n * SIDE:] = db[:, q * SIDE:(q + 1) * SIDE]
    mine_at = k * T + t
    in_plane(lambda kk, u: remote(piece.at[kk * T + u], piece_in.at[mine_at], x_send, x_recv, kk * Z + z, u))
    piece_in[mine_at] = piece[mine_at]
    each(T - 1, lambda o: remote(nbuf.at[mine], nbuf.at[mine], n_send, n_recv, r, rem(t + o, T)), 1)
    rest = piece_in.at[pl.ds(0, 2 * T - 1)]
    wait_bytes(rest, x_recv)
    lined[z] = jnp.sum(piece_in[...], axis=0)
    each(Z - 1, lambda o: remote(lined.at[z], lined.at[z], d_send, d_recv, k * Z + rem(z + o, Z), t), 1)

    wait_bytes(nbuf.at[pl.ds(0, (T - 1) * PR)], n_recv)
    for b in range(blocks):
        span = pl.ds(b * SIDE, SIDE)
        pre, gate = layer(nbuf[span, :])
        act_out[span, :] = (pre * gate).astype(BF16)
    wait_bytes(lined.at[pl.ds(0, Z - 1)], d_recv)
    final[mine_at] = jnp.sum(lined[...], axis=0)
    in_plane(lambda kk, u: remote(final.at[mine_at], final.at[mine_at], e_send, e_recv, kk * Z + z, u))

    wait_bytes(up.at[pl.ds(1, Z // 2)], up_send)
    wait_bytes(dn.at[pl.ds(1, Z // 2 - 1)], dn_send)
    wait_bytes(table.at[pl.ds(0, (2 * T - 1) * PR)], a2_send)
    wait_bytes(degr, g_send)
    wait_bytes(aggr, p_send)
    wait_bytes(nbuf.at[pl.ds(0, (T - 1) * PR)], n_send)
    wait_bytes(rest, x_send)
    wait_bytes(lined.at[pl.ds(0, Z - 1)], d_send)
    wait_bytes(rest, e_send)
    wait_bytes(rest, e_recv)
    for u in range(T):
        for q in range(2):
            for j in range(n):
                i = u * SR + q * HR + j // 2
                dw_out[i:i + 1, (j % 2) * SIDE:(j % 2 + 1) * SIDE] = final[q * T + u, :, j * SIDE:(j + 1) * SIDE]
    for q in range(2):
        db_out[:, q * SIDE:(q + 1) * SIDE] = final[q * T, :, n * SIDE:]


def hand_out(a, b, c, a_out, b_out, c_out, a_sem, b_sem, c_sem):
    copies = [pltpu.make_async_copy(*x) for x in ((a, a_out, a_sem), (b, b_out, b_sem), (c, c_out, c_sem))]
    for copy in copies:
        copy.start()
    for copy in copies:
        copy.wait()


def per_device(T, Z, features, tile_vals, tile_row, tile_col, tile_count, weight, bias, cotangent):
    rows, width = features.shape
    slots = tile_vals.shape[2]
    hidden = weight.shape[1]
    PR = rows // T
    SR = SIDE // T
    line = (SR + 1) * SIDE
    any_spec = pl.BlockSpec(memory_space=pl.ANY)
    vmem = pl.BlockSpec(memory_space=pltpu.VMEM)
    dma = pltpu.SemaphoreType.DMA
    V = pltpu.VMEM
    out_shape = (
        jax.ShapeDtypeStruct((rows, hidden), BF16),
        jax.ShapeDtypeStruct((width, hidden), F32),
        jax.ShapeDtypeStruct((1, hidden), F32),
    )
    results = pl.pallas_call(
        functools.partial(kernel, T, Z),
        out_shape=tuple(V(x.shape, x.dtype) for x in out_shape),
        in_specs=[any_spec] * 8,
        out_specs=(vmem,) * 3,
        scratch_shapes=[
            V((slots, SIDE, SIDE), BF16),
            V((Z // 2 + 1, PR, width), BF16),
            V((Z // 2, PR, width), BF16),
            V((2 * rows, width), BF16),
            V((slots + 1, SIDE, SIDE), BF16),
            V((slots + 1, SIDE, SIDE), BF16),
            V((SIDE, SIDE), F32),
            V((8, SIDE), jnp.int32),
            pltpu.SMEM((8, SIDE), jnp.int32),
            V((1, slots), jnp.int32),
            V((1, slots), jnp.int32),
            pltpu.SMEM((1, 1), jnp.int32),
            V((rows, width), F32),
            V((rows, width), BF16),
            V((rows, SIDE), F32),
            V((rows, SIDE), BF16),
            V((T - 1, PR, SIDE), BF16),
            V((T - 1, PR, width), BF16),
            V((rows, width), BF16),
            V((width, hidden), BF16),
            V((1, hidden), F32),
            V((rows, hidden), BF16),
            V((2 * T, 1, line), F32),
            V((2 * T, 1, line), F32),
            V((Z, 1, line), F32),
            V((2 * T, 1, line), F32),
        ]
        + [dma] * 8
        + [dma, dma((Z // 2 + 1,)), dma, dma((Z // 2 + 1,))]
        + [dma] * 14,
        compiler_params=pltpu.CompilerParams(
            collective_id=0, has_side_effects=True, vmem_limit_bytes=56 * 1024 * 1024
        ),
        cost_estimate=pl.CostEstimate(
            flops=2 * slots * SIDE * SIDE * width, bytes_accessed=2 * slots * SIDE * SIDE, transcendentals=rows * hidden
        ),
    )(
        features,
        tile_vals.reshape(slots, SIDE, SIDE),
        tile_row.reshape(1, slots),
        tile_col.reshape(1, slots),
        tile_count,
        weight,
        bias.reshape(1, hidden),
        cotangent,
    )
    activated, dw, db = pl.pallas_call(
        hand_out,
        out_shape=out_shape,
        in_specs=[vmem] * 3,
        out_specs=(any_spec,) * 3,
        scratch_shapes=[dma] * 3,
        compiler_params=pltpu.CompilerParams(vmem_limit_bytes=56 * 1024 * 1024),
    )(*(pltpu.with_memory_space_constraint(x, pltpu.VMEM) for x in results))
    return activated, dw, db.reshape(hidden)


def solution(mesh):
    in_specs = (
        P("row", None),
        P("row", "team", None, None, None),
        P("row", "team", None),
        P("row", "team", None),
        P("row", "team"),
        P(),
        P(),
        P("row", None),
    )
    out_specs = (P("row", None), P(), P())
    T = mesh.shape["team"]
    Z = mesh.shape["row"] // 2
    return jax.shard_map(
        functools.partial(per_device, T, Z), mesh=mesh, in_specs=in_specs, out_specs=out_specs, check_vma=False
    )
```

time: 624 us -> 55.8 us (0.09)
  the two profiles are of different devices: /device:TPU:24 before, /device:TPU:1 now
where the time goes in v2:
time: 55.8 us; the launch traced here: 55.6 us
  Pallas kernels  54.4 us (97%)
  between operations  1.29 us (2%)
    pallas_call x1, Pallas kernels, per_device(): pl.pallas_call(functools.partial(kernel, T, Z), out_shape=tuple((V(x.shap...  53.6 us

profile of v2, /device:TPU:1, one launch (start us, length us, event | category | flops | bytes accessed | tf_op | source)
XLA Modules:
  0.0 55.6 jit_solution(12520282825245340054)
XLA Ops:
  1.3 53.6 %shard_map.103 = (bf16[512,256]{1,0:T(8,128)(2,1)S(1)}, f32[128,256]{1,0:T(8,128)S(1)}, f32[1,256]{1,0:T(1,128)S(1)}) custom-call(bf16[512,128]{1,0:T(8,128)(2,1)} %feat.1, bf16[128,128,128]{2,1,0:T(8,128)(2,1)} %bitcast.5, s32[1,128]{1,0:T(1,128)} %bitcast.7, s32[1,128]{1,0:T(1,128)} %bitcast.8, s32[1,1]{1,0:T(1,128)S(6)} %copy.11.tcount, ...), custom_call_target="tpu_custom_call" | custom-call | flops 536870912 | bytes 4194304 | tf_op jit(solution)/shard_map/pallas_call | solution.py:320
  54.9 0.8 %shard_map.104 = (bf16[512,256]{1,0:T(8,128)(2,1)}, f32[128,256]{1,0:T(8,128)}, f32[1,256]{1,0:T(1,128)}) custom-call(bf16[512,256]{1,0:T(8,128)(2,1)S(1)} %get-tuple-element.9.a, f32[128,256]{1,0:T(8,128)S(1)} %get-tuple-element.10.b, f32[1,256]{1,0:T(1,128)S(1)} %get-tuple-element.11.c), custom_call_target="tpu_custom_call" | custom-call | tf_op jit(solution)/shard_map/pallas_call | solution.py:372

commit v3 on v2

--- a/solution.py
+++ b/solution.py
@@ -32,7 +32,7 @@
     T, Z, feat, tiles, trow, tcol, tcount, weight, bias, cot,
     act_out, dw_out, db_out,
     a_vm, up, dn, table, high, low, running, order_v, order, row_v, col_v, count_s,
-    agg, aggs, deg, degs, degr, aggr, nbuf, w_vm, b_vm, c_vm,
+    agg, aggs, degs, degr, aggr, nbuf, w_vm, b_vm, c_vm,
     piece, piece_in, lined, final,
     tile_sem, row_sem, col_sem, count_sem, order_sem, w_sem, b_sem, c_sem,
     up_send, up_recv, dn_send, dn_recv, a2_send, a2_recv, g_send, g_recv, p_send, p_recv,
@@ -82,13 +82,9 @@
     count_copy.start()
     mine = pl.ds(pl.multiple_of(t * PR, PR), PR)
     tile_copy = pltpu.make_async_copy(tiles, a_vm, tile_sem)
-    tile_copy.start()
     w_copy = pltpu.make_async_copy(weight, w_vm, w_sem)
     b_copy = pltpu.make_async_copy(bias, b_vm, b_sem)
     c_copy = pltpu.make_async_copy(cot, c_vm, c_sem)
-    w_copy.start()
-    b_copy.start()
-    c_copy.start()
 
     pl.semaphore_wait(barrier, len(near) + 2 * T - 1)
 
@@ -126,6 +122,7 @@
                     forward(buf.at[d], rem(z - sign * d + Z, Z))
 
     forward(own_piece, z)
+    tile_copy.start()
 
     row_copy.wait()
     col_copy.wait()
@@ -159,6 +156,9 @@
     low[slots] = jnp.zeros((SIDE, SIDE), BF16)
     running[...] = jnp.zeros_like(running)
     relay()
+    w_copy.start()
+    b_copy.start()
+    c_copy.start()
     pass_on(range(S, 0, -1))
     order_copy.wait()
     tile_copy.wait()
@@ -191,18 +191,17 @@
         return got + jnp.dot(dense(low, half), right, preferred_element_type=F32)
 
     pair = 2 * SIDE
-    left_lanes = lax.broadcasted_iota(jnp.int32, (pair, SIDE), 1) < SIDE // 2
+    across_lane = lax.broadcasted_iota(jnp.int32, (SIDE, SIDE), 1)
+    down_line = lax.broadcasted_iota(jnp.int32, (SIDE, SIDE), 0)
     for half in range(blocks // 2):
-        span = pl.ds(half * pair, pair)
         sums = product(half, jnp.ones((wide * SIDE, SIDE), BF16))
-        top = sums.astype(BF16).astype(F32)
-        deg[span, :] = sums
-        degs[span, :] = jnp.where(left_lanes, top, sums - top).astype(BF16)
+        for j in range(2):
+            square = jnp.where(across_lane == down_line, sums[j * SIDE:(j + 1) * SIDE, :], 0.0)
+            degs[2 * half + j] = jnp.sum(square, axis=0, keepdims=True)
 
     def give_degree(o):
         u = rem(t + o, T)
-        part = pl.ds(pl.multiple_of(u * PR, PR), PR)
-        remote(degs.at[part], degr.at[o - 1], g_send, g_recv, r, u)
+        remote(degs.at[lax.div(u * PR, SIDE)], degr.at[o - 1], g_send, g_recv, r, u)
 
     each(T - 1, give_degree, 1)
     wait_bytes(table, a2_recv)
@@ -223,10 +222,10 @@
         each(owners, give_part, half * owners)
 
     wait_bytes(degr, g_recv)
-    degree = degr[0].astype(F32)
-    for o in range(1, T - 1):
-        degree += degr[o].astype(F32)
-    degree = jnp.sum(degree, axis=1, keepdims=True) * (2.0 / SIDE) + deg[mine, :] + 1.0
+    degree = degs[lax.div(t * PR, SIDE)] + jnp.sum(degr[...], axis=0) + 1.0
+    here = lax.broadcasted_iota(jnp.int32, (PR, SIDE), 0) + rem(t * PR, SIDE)
+    here = here == lax.broadcasted_iota(jnp.int32, (PR, SIDE), 1)
+    degree = jnp.sum(jnp.where(here, degree, 0.0), axis=1, keepdims=True)
     root = jnp.sqrt(degree)
     wait_bytes(aggr, p_recv)
     total = agg[mine, :]
@@ -259,20 +258,20 @@
     mine_at = k * T + t
     in_plane(lambda kk, u: remote(piece.at[kk * T + u], piece_in.at[mine_at], x_send, x_recv, kk * Z + z, u))
     piece_in[mine_at] = piece[mine_at]
-    each(T - 1, lambda o: remote(nbuf.at[mine], nbuf.at[mine], n_send, n_recv, r, rem(t + o, T)), 1)
     rest = piece_in.at[pl.ds(0, 2 * T - 1)]
     wait_bytes(rest, x_recv)
     lined[z] = jnp.sum(piece_in[...], axis=0)
     each(Z - 1, lambda o: remote(lined.at[z], lined.at[z], d_send, d_recv, k * Z + rem(z + o, Z), t), 1)
+    each(T - 1, lambda o: remote(nbuf.at[mine], nbuf.at[mine], n_send, n_recv, r, rem(t + o, T)), 1)
+    wait_bytes(lined.at[pl.ds(0, Z - 1)], d_recv)
+    final[mine_at] = jnp.sum(lined[...], axis=0)
+    in_plane(lambda kk, u: remote(final.at[mine_at], final.at[mine_at], e_send, e_recv, kk * Z + z, u))
 
     wait_bytes(nbuf.at[pl.ds(0, (T - 1) * PR)], n_recv)
     for b in range(blocks):
         span = pl.ds(b * SIDE, SIDE)
         pre, gate = layer(nbuf[span, :])
         act_out[span, :] = (pre * gate).astype(BF16)
-    wait_bytes(lined.at[pl.ds(0, Z - 1)], d_recv)
-    final[mine_at] = jnp.sum(lined[...], axis=0)
-    in_plane(lambda kk, u: remote(final.at[mine_at], final.at[mine_at], e_send, e_recv, kk * Z + z, u))
 
     wait_bytes(up.at[pl.ds(1, Z // 2)], up_send)
     wait_bytes(dn.at[pl.ds(1, Z // 2 - 1)], dn_send)
@@ -337,9 +336,8 @@
             pltpu.SMEM((1, 1), jnp.int32),
             V((rows, width), F32),
             V((rows, width), BF16),
-            V((rows, SIDE), F32),
-            V((rows, SIDE), BF16),
-            V((T - 1, PR, SIDE), BF16),
+            V((rows // SIDE, 1, SIDE), F32),
+            V((T - 1, 1, SIDE), F32),
             V((T - 1, PR, width), BF16),
             V((rows, width), BF16),
             V((width, hidden), BF16),

time: 55.8 us -> 55.2 us (0.989)
  Pallas kernels: 54.4 us -> 53.7 us
    pallas_call x1, Pallas kernels: 53.6 us -> 53 us  [per_device(): pl.pallas_call(functools.partial(kernel, T, Z), out_shape=tuple((V(x.shap...]
where the time goes in v3:
time: 55.2 us; the launch traced here: 55 us
  Pallas kernels  53.7 us (97%)
  between operations  1.29 us (2%)
    pallas_call x1, Pallas kernels, per_device(): pl.pallas_call(functools.partial(kernel, T, Z), out_shape=tuple((V(x.shap...  53 us

profile of v3, /device:TPU:1, one launch (start us, length us, event | category | flops | bytes accessed | tf_op | source)
XLA Modules:
  0.0 55.0 jit_solution(6129388520022913804)
XLA Ops:
  1.3 53.0 %shard_map.103 = (bf16[512,256]{1,0:T(8,128)(2,1)S(1)}, f32[128,256]{1,0:T(8,128)S(1)}, f32[1,256]{1,0:T(1,128)S(1)}) custom-call(bf16[512,128]{1,0:T(8,128)(2,1)} %feat.1, bf16[128,128,128]{2,1,0:T(8,128)(2,1)} %bitcast.5, s32[1,128]{1,0:T(1,128)} %bitcast.7, s32[1,128]{1,0:T(1,128)} %bitcast.8, s32[1,1]{1,0:T(1,128)S(6)} %copy.11.tcount, ...), custom_call_target="tpu_custom_call" | custom-call | flops 536870912 | bytes 4194304 | tf_op jit(solution)/shard_map/pallas_call | solution.py:319
  54.3 0.8 %shard_map.104 = (bf16[512,256]{1,0:T(8,128)(2,1)}, f32[128,256]{1,0:T(8,128)}, f32[1,256]{1,0:T(1,128)}) custom-call(bf16[512,256]{1,0:T(8,128)(2,1)S(1)} %get-tuple-element.9.a, f32[128,256]{1,0:T(8,128)S(1)} %get-tuple-element.10.b, f32[1,256]{1,0:T(1,128)S(1)} %get-tuple-element.11.c), custom_call_target="tpu_custom_call" | custom-call | tf_op jit(solution)/shard_map/pallas_call | solution.py:370

commit v4 on v3

--- a/solution.py
+++ b/solution.py
@@ -32,10 +32,10 @@
     T, Z, feat, tiles, trow, tcol, tcount, weight, bias, cot,
     act_out, dw_out, db_out,
     a_vm, up, dn, table, high, low, running, order_v, order, row_v, col_v, count_s,
-    agg, aggs, degs, degr, aggr, nbuf, w_vm, b_vm, c_vm,
+    agg, aggs, aggr, nbuf, w_vm, b_vm, c_vm,
     piece, piece_in, lined, final,
     tile_sem, row_sem, col_sem, count_sem, order_sem, w_sem, b_sem, c_sem,
-    up_send, up_recv, dn_send, dn_recv, a2_send, a2_recv, g_send, g_recv, p_send, p_recv,
+    up_send, up_recv, dn_send, dn_recv, a2_send, a2_recv, p_send, p_recv,
     n_send, n_recv, x_send, x_recv, d_send, d_recv, e_send, e_recv,
 ):
     R = 2 * Z
@@ -176,9 +176,10 @@
         running[...] = held
 
     chunks = slots // chunk
-    pl.loop(0, chunks // 2)(sum_tiles)
+    early = 3 * chunks // 8
+    pl.loop(0, early)(sum_tiles)
     pass_on(range(Z // 2, S, -1))
-    pl.loop(chunks // 2, chunks)(sum_tiles)
+    pl.loop(early, chunks)(sum_tiles)
 
     def dense(part, half):
         bands = []
@@ -190,47 +191,38 @@
         got = jnp.dot(dense(high, half), right, preferred_element_type=F32)
         return got + jnp.dot(dense(low, half), right, preferred_element_type=F32)
 
+    wait_bytes(table, a2_recv)
+
     pair = 2 * SIDE
-    across_lane = lax.broadcasted_iota(jnp.int32, (SIDE, SIDE), 1)
-    down_line = lax.broadcasted_iota(jnp.int32, (SIDE, SIDE), 0)
+    owners = pair // PR
+    PD = PR // 2
+    quarter = lax.broadcasted_iota(jnp.int32, (PD, SIDE), 1) // (SIDE // 4)
+    right = jnp.concatenate([table[...], jnp.ones((wide * SIDE, SIDE), BF16)], axis=1)
     for half in range(blocks // 2):
-        sums = product(half, jnp.ones((wide * SIDE, SIDE), BF16))
-        for j in range(2):
-            square = jnp.where(across_lane == down_line, sums[j * SIDE:(j + 1) * SIDE, :], 0.0)
-            degs[2 * half + j] = jnp.sum(square, axis=0, keepdims=True)
-
-    def give_degree(o):
-        u = rem(t + o, T)
-        remote(degs.at[lax.div(u * PR, SIDE)], degr.at[o - 1], g_send, g_recv, r, u)
-
-    each(T - 1, give_degree, 1)
-    wait_bytes(table, a2_recv)
-
-    owners = pair // PR
-    for half in range(blocks // 2):
-        span = pl.ds(half * pair, pair)
-        got = product(half, table[...])
-        agg[span, :] = got
-        aggs[span, :] = got.astype(BF16)
+        got = product(half, right)
+        agg[pl.ds(half * pair, pair), :] = got[:, :SIDE]
+        for v in range(owners):
+            u = half * owners + v
+            aggs[u, 0:PR, :] = got[v * PR:(v + 1) * PR, :SIDE].astype(BF16)
+            sums = jnp.where(quarter < 2, got[v * PR:v * PR + PD, SIDE:], got[v * PR + PD:(v + 1) * PR, SIDE:])
+            top = sums.astype(BF16).astype(F32)
+            aggs[u, PR:, :] = jnp.where((quarter == 0) | (quarter == 2), top, sums - top).astype(BF16)
 
         def give_part(u):
             @pl.when(u != t)
             def _():
-                part = pl.ds(pl.multiple_of(u * PR, PR), PR)
-                remote(aggs.at[part], aggr.at[rem(u - t + T, T) - 1], p_send, p_recv, r, u)
+                remote(aggs.at[u], aggr.at[rem(u - t + T, T) - 1], p_send, p_recv, r, u)
 
         each(owners, give_part, half * owners)
 
-    wait_bytes(degr, g_recv)
-    degree = degs[lax.div(t * PR, SIDE)] + jnp.sum(degr[...], axis=0) + 1.0
-    here = lax.broadcasted_iota(jnp.int32, (PR, SIDE), 0) + rem(t * PR, SIDE)
-    here = here == lax.broadcasted_iota(jnp.int32, (PR, SIDE), 1)
-    degree = jnp.sum(jnp.where(here, degree, 0.0), axis=1, keepdims=True)
-    root = jnp.sqrt(degree)
     wait_bytes(aggr, p_recv)
     total = agg[mine, :]
+    parts = aggs[t, PR:, :].astype(F32)
     for o in range(T - 1):
-        total += aggr[o].astype(F32)
+        total += aggr[o, 0:PR, :].astype(F32)
+        parts += aggr[o, PR:, :].astype(F32)
+    ends = [jnp.sum(jnp.where(quarter // 2 == q, parts, 0.0), axis=1, keepdims=True) for q in range(2)]
+    root = jnp.sqrt(jnp.concatenate(ends, axis=0) * (4.0 / SIDE) + 1.0)
     w_copy.wait()
     b_copy.wait()
     c_copy.wait()
@@ -276,7 +268,6 @@
     wait_bytes(up.at[pl.ds(1, Z // 2)], up_send)
     wait_bytes(dn.at[pl.ds(1, Z // 2 - 1)], dn_send)
     wait_bytes(table.at[pl.ds(0, (2 * T - 1) * PR)], a2_send)
-    wait_bytes(degr, g_send)
     wait_bytes(aggr, p_send)
     wait_bytes(nbuf.at[pl.ds(0, (T - 1) * PR)], n_send)
     wait_bytes(rest, x_send)
@@ -335,10 +326,8 @@
             V((1, slots), jnp.int32),
             pltpu.SMEM((1, 1), jnp.int32),
             V((rows, width), F32),
-            V((rows, width), BF16),
-            V((rows // SIDE, 1, SIDE), F32),
-            V((T - 1, 1, SIDE), F32),
-            V((T - 1, PR, width), BF16),
+            V((T, PR + PR // 2, width), BF16),
+            V((T - 1, PR + PR // 2, width), BF16),
             V((rows, width), BF16),
             V((width, hidden), BF16),
             V((1, hidden), F32),
@@ -350,7 +339,7 @@
         ]
         + [dma] * 8
         + [dma, dma((Z // 2 + 1,)), dma, dma((Z // 2 + 1,))]
-        + [dma] * 14,
+        + [dma] * 12,
         compiler_params=pltpu.CompilerParams(
             collective_id=0, has_side_effects=True, vmem_limit_bytes=56 * 1024 * 1024
         ),

time: 55.2 us -> 56.2 us (1.018)
  Pallas kernels: 53.7 us -> 54.8 us
    pallas_call x1, Pallas kernels: 53 us -> 54 us  [per_device(): pl.pallas_call(functools.partial(kernel, T, Z), out_shape=tuple((V(x.shap...]
where the time goes in v4:
time: 56.2 us; the launch traced here: 56 us
  Pallas kernels  54.8 us (98%)
  between operations  1.29 us (2%)
    pallas_call x1, Pallas kernels, per_device(): pl.pallas_call(functools.partial(kernel, T, Z), out_shape=tuple((V(x.shap...  54 us

profile of v4, /device:TPU:1, one launch (start us, length us, event | category | flops | bytes accessed | tf_op | source)
XLA Modules:
  0.0 56.0 jit_solution(10627584083210180396)
XLA Ops:
  1.3 54.0 %shard_map.103 = (bf16[512,256]{1,0:T(8,128)(2,1)S(1)}, f32[128,256]{1,0:T(8,128)S(1)}, f32[1,256]{1,0:T(1,128)S(1)}) custom-call(bf16[512,128]{1,0:T(8,128)(2,1)} %feat.1, bf16[128,128,128]{2,1,0:T(8,128)(2,1)} %bitcast.5, s32[1,128]{1,0:T(1,128)} %bitcast.7, s32[1,128]{1,0:T(1,128)} %bitcast.8, s32[1,1]{1,0:T(1,128)S(6)} %copy.11.tcount, ...), custom_call_target="tpu_custom_call" | custom-call | flops 536870912 | bytes 4194304 | tf_op jit(solution)/shard_map/pallas_call | solution.py:310
  55.3 0.8 %shard_map.104 = (bf16[512,256]{1,0:T(8,128)(2,1)}, f32[128,256]{1,0:T(8,128)}, f32[1,256]{1,0:T(1,128)}) custom-call(bf16[512,256]{1,0:T(8,128)(2,1)S(1)} %get-tuple-element.9.a, f32[128,256]{1,0:T(8,128)S(1)} %get-tuple-element.10.b, f32[1,256]{1,0:T(1,128)S(1)} %get-tuple-element.11.c), custom_call_target="tpu_custom_call" | custom-call | tf_op jit(solution)/shard_map/pallas_call | solution.py:359

commit v5 on v3

--- a/solution.py
+++ b/solution.py
@@ -33,10 +33,10 @@
     act_out, dw_out, db_out,
     a_vm, up, dn, table, high, low, running, order_v, order, row_v, col_v, count_s,
     agg, aggs, degs, degr, aggr, nbuf, w_vm, b_vm, c_vm,
-    piece, piece_in, lined, final,
+    piece, piece_in, lined, bias_line, final,
     tile_sem, row_sem, col_sem, count_sem, order_sem, w_sem, b_sem, c_sem,
     up_send, up_recv, dn_send, dn_recv, a2_send, a2_recv, g_send, g_recv, p_send, p_recv,
-    n_send, n_recv, x_send, x_recv, d_send, d_recv, e_send, e_recv,
+    n_send, n_recv, x_send, x_recv, b_send, b_recv, d_send, d_recv, e_send, e_recv,
 ):
     R = 2 * Z
     slots = a_vm.shape[0]
@@ -249,22 +249,49 @@
     SR = SIDE // T
     HR = SR // 2
     n = 2 * HR
+    mine_at = k * T + t
     for q in range(2):
         for u in range(T):
             for j in range(n):
                 i = u * SR + q * HR + j // 2
                 piece[q * T + u, :, j * SIDE:(j + 1) * SIDE] = dw[i:i + 1, (j % 2) * SIDE:(j % 2 + 1) * SIDE]
             piece[q * T + u, :, n * SIDE:] = db[:, q * SIDE:(q + 1) * SIDE]
-    mine_at = k * T + t
-    in_plane(lambda kk, u: remote(piece.at[kk * T + u], piece_in.at[mine_at], x_send, x_recv, kk * Z + z, u))
+
+        def give_line(u):
+            remote(piece.at[q * T + u], piece_in.at[mine_at], x_send, x_recv, q * Z + z, u)
+
+        @pl.when(k != q)
+        def _():
+            give_line(t)
+
+        each(T - 1, lambda o: give_line(rem(t + o, T)), 1)
     piece_in[mine_at] = piece[mine_at]
     rest = piece_in.at[pl.ds(0, 2 * T - 1)]
     wait_bytes(rest, x_recv)
-    lined[z] = jnp.sum(piece_in[...], axis=0)
+    plane = jnp.sum(piece_in[...], axis=0)
+    lined[z] = jnp.concatenate([plane[:, j * SIDE:(j + 1) * SIDE] for j in range(n)], axis=0).astype(BF16)
+    bias_line[0] = plane[:, n * SIDE:]
+
+    @pl.when(t != 0)
+    def _():
+        remote(bias_line.at[0], bias_line.at[1], b_send, b_recv, k * Z + rem(z + t, Z), t)
+
+    @pl.when(t == 0)
+    def _():
+        bias_line[1] = plane[:, n * SIDE:]
+
     each(Z - 1, lambda o: remote(lined.at[z], lined.at[z], d_send, d_recv, k * Z + rem(z + o, Z), t), 1)
     each(T - 1, lambda o: remote(nbuf.at[mine], nbuf.at[mine], n_send, n_recv, r, rem(t + o, T)), 1)
     wait_bytes(lined.at[pl.ds(0, Z - 1)], d_recv)
-    final[mine_at] = jnp.sum(lined[...], axis=0)
+    half_slice = jnp.sum(lined[...].astype(F32), axis=0)
+    for j in range(n):
+        final[mine_at, :, j * SIDE:(j + 1) * SIDE] = half_slice[j:j + 1, :]
+
+    @pl.when(t != 0)
+    def _():
+        wait_bytes(bias_line.at[1], b_recv)
+
+    final[mine_at, :, n * SIDE:] = bias_line[1]
     in_plane(lambda kk, u: remote(final.at[mine_at], final.at[mine_at], e_send, e_recv, kk * Z + z, u))
 
     wait_bytes(nbuf.at[pl.ds(0, (T - 1) * PR)], n_recv)
@@ -280,6 +307,11 @@
     wait_bytes(aggr, p_send)
     wait_bytes(nbuf.at[pl.ds(0, (T - 1) * PR)], n_send)
     wait_bytes(rest, x_send)
+
+    @pl.when(t != 0)
+    def _():
+        wait_bytes(bias_line.at[0], b_send)
+
     wait_bytes(lined.at[pl.ds(0, Z - 1)], d_send)
     wait_bytes(rest, e_send)
     wait_bytes(rest, e_recv)
@@ -289,7 +321,10 @@
                 i = u * SR + q * HR + j // 2
                 dw_out[i:i + 1, (j % 2) * SIDE:(j % 2 + 1) * SIDE] = final[q * T + u, :, j * SIDE:(j + 1) * SIDE]
     for q in range(2):
-        db_out[:, q * SIDE:(q + 1) * SIDE] = final[q * T, :, n * SIDE:]
+        db = final[q * T + z, :, n * SIDE:]
+        for p in range(1, Z):
+            db += final[q * T + rem(z - p + Z, Z), :, n * SIDE:]
+        db_out[:, q * SIDE:(q + 1) * SIDE] = db
 
 
 def hand_out(a, b, c, a_out, b_out, c_out, a_sem, b_sem, c_sem):
@@ -345,12 +380,13 @@
             V((rows, hidden), BF16),
             V((2 * T, 1, line), F32),
             V((2 * T, 1, line), F32),
-            V((Z, 1, line), F32),
+            V((Z, SR, SIDE), BF16),
+            V((2, 1, SIDE), F32),
             V((2 * T, 1, line), F32),
         ]
         + [dma] * 8
         + [dma, dma((Z // 2 + 1,)), dma, dma((Z // 2 + 1,))]
-        + [dma] * 14,
+        + [dma] * 16,
         compiler_params=pltpu.CompilerParams(
             collective_id=0, has_side_effects=True, vmem_limit_bytes=56 * 1024 * 1024
         ),

time: 55.2 us -> 54.8 us (level)
  no operation moved by 1% of the time
where the time goes in v5:
time: 54.8 us; the launch traced here: 54.7 us
  Pallas kernels  53.4 us (97%)
  between operations  1.29 us (2%)
    pallas_call x1, Pallas kernels, per_device(): pl.pallas_call(functools.partial(kernel, T, Z), out_shape=tuple((V(x.shap...  52.6 us

profile of v5, /device:TPU:1, one launch (start us, length us, event | category | flops | bytes accessed | tf_op | source)
XLA Modules:
  0.0 54.7 jit_solution(18372389493166325752)
XLA Ops:
  1.3 52.6 %shard_map.103 = (bf16[512,256]{1,0:T(8,128)(2,1)S(1)}, f32[128,256]{1,0:T(8,128)S(1)}, f32[1,256]{1,0:T(1,128)S(1)}) custom-call(bf16[512,128]{1,0:T(8,128)(2,1)} %feat.1, bf16[128,128,128]{2,1,0:T(8,128)(2,1)} %bitcast.5, s32[1,128]{1,0:T(1,128)} %bitcast.7, s32[1,128]{1,0:T(1,128)} %bitcast.8, s32[1,1]{1,0:T(1,128)S(6)} %copy.11.tcount, ...), custom_call_target="tpu_custom_call" | custom-call | flops 536870912 | bytes 4194304 | tf_op jit(solution)/shard_map/pallas_call | solution.py:354
  53.9 0.8 %shard_map.104 = (bf16[512,256]{1,0:T(8,128)(2,1)}, f32[128,256]{1,0:T(8,128)}, f32[1,256]{1,0:T(1,128)}) custom-call(bf16[512,256]{1,0:T(8,128)(2,1)S(1)} %get-tuple-element.9.a, f32[128,256]{1,0:T(8,128)S(1)} %get-tuple-element.10.b, f32[1,256]{1,0:T(1,128)S(1)} %get-tuple-element.11.c), custom_call_target="tpu_custom_call" | custom-call | tf_op jit(solution)/shard_map/pallas_call | solution.py:406

commit v6 on v5

--- a/solution.py
+++ b/solution.py
@@ -55,8 +55,6 @@
         ).start()
 
     barrier = pltpu.get_barrier_semaphore()
-    S = Z // 4
-    near = [*range(1, S + 1), *range(Z - S, Z)]
 
     def signal(row, team):
         pl.semaphore_signal(barrier, inc=1, device_id={"row": row, "team": team}, device_id_type=MESH)
@@ -70,8 +68,7 @@
         body(1 - k, t)
         each(T - 1, both, 1)
 
-    for o in near:
-        signal(k * Z + rem(z + o, Z), t)
+    each(Z - 1, lambda o: signal(k * Z + rem(z + o, Z), t), 1)
     in_plane(lambda kk, u: signal(kk * Z + z, u))
 
     row_copy = pltpu.make_async_copy(trow, row_v, row_sem)
@@ -86,12 +83,14 @@
     b_copy = pltpu.make_async_copy(bias, b_vm, b_sem)
     c_copy = pltpu.make_async_copy(cot, c_vm, c_sem)
 
-    pl.semaphore_wait(barrier, len(near) + 2 * T - 1)
+    pl.semaphore_wait(barrier, Z - 1 + 2 * T - 1)
 
     ways = ((up, up_send, up_recv, 1, Z // 2), (dn, dn_send, dn_recv, -1, Z // 2 - 1))
     own_piece = feat.at[mine]
-    for d in range(S, 0, -1):
+    for d in range(Z // 2, 0, -1):
         for buf, ssem, rsem, sign, far in ways:
+            if d > far:
+                continue
             remote(own_piece, buf.at[d], ssem, rsem.at[d], k * Z + rem(z + sign * d + Z, Z), t)
 
     place = pl.ds(pl.multiple_of((k * T + t) * PR, PR), PR)
@@ -106,19 +105,12 @@
         @pl.when(source == t)
         def _():
             pltpu.make_async_copy(piece_ref, table.at[place], a2_recv).start()
-
-    def relay():
-        for buf, ssem, rsem, sign, far in ways:
-            wait_bytes(buf.at[S], rsem.at[S])
-            for e in range(far - S, 0, -1):
-                remote(buf.at[S], buf.at[S + e], ssem, rsem.at[S + e], k * Z + rem(z + sign * e + Z, Z), t)
 
     def pass_on(distances):
         for d in distances:
             for buf, ssem, rsem, sign, far in ways:
                 if d <= far:
-                    if d != S:
-                        wait_bytes(buf.at[d], rsem.at[d])
+                    wait_bytes(buf.at[d], rsem.at[d])
                     forward(buf.at[d], rem(z - sign * d + Z, Z))
 
     forward(own_piece, z)
@@ -155,11 +147,10 @@
     high[slots] = jnp.zeros((SIDE, SIDE), BF16)
     low[slots] = jnp.zeros((SIDE, SIDE), BF16)
     running[...] = jnp.zeros_like(running)
-    relay()
+    pass_on(range(Z // 2, Z // 4, -1))
     w_copy.start()
     b_copy.start()
     c_copy.start()
-    pass_on(range(S, 0, -1))
     order_copy.wait()
     tile_copy.wait()
 
@@ -177,7 +168,7 @@
 
     chunks = slots // chunk
     pl.loop(0, chunks // 2)(sum_tiles)
-    pass_on(range(Z // 2, S, -1))
+    pass_on(range(Z // 4, 0, -1))
     pl.loop(chunks // 2, chunks)(sum_tiles)
 
     def dense(part, half):

time: 54.8 us -> 57.5 us (1.049)
  Pallas kernels: 53.4 us -> 56.1 us
    pallas_call x1, Pallas kernels: 52.6 us -> 55.3 us  [per_device(): pl.pallas_call(functools.partial(kernel, T, Z), out_shape=tuple((V(x.shap...]
where the time goes in v6:
time: 57.5 us; the launch traced here: 57.3 us
  Pallas kernels  56.1 us (98%)
  between operations  1.29 us (2%)
    pallas_call x1, Pallas kernels, per_device(): pl.pallas_call(functools.partial(kernel, T, Z), out_shape=tuple((V(x.shap...  55.3 us

profile of v6, /device:TPU:1, one launch (start us, length us, event | category | flops | bytes accessed | tf_op | source)
XLA Modules:
  0.0 57.3 jit_solution(11465600550622501252)
XLA Ops:
  1.3 55.3 %shard_map.103 = (bf16[512,256]{1,0:T(8,128)(2,1)S(1)}, f32[128,256]{1,0:T(8,128)S(1)}, f32[1,256]{1,0:T(1,128)S(1)}) custom-call(bf16[512,128]{1,0:T(8,128)(2,1)} %feat.1, bf16[128,128,128]{2,1,0:T(8,128)(2,1)} %bitcast.5, s32[1,128]{1,0:T(1,128)} %bitcast.7, s32[1,128]{1,0:T(1,128)} %bitcast.8, s32[1,1]{1,0:T(1,128)S(6)} %copy.11.tcount, ...), custom_call_target="tpu_custom_call" | custom-call | flops 536870912 | bytes 4194304 | tf_op jit(solution)/shard_map/pallas_call | solution.py:345
  56.6 0.8 %shard_map.104 = (bf16[512,256]{1,0:T(8,128)(2,1)}, f32[128,256]{1,0:T(8,128)}, f32[1,256]{1,0:T(1,128)}) custom-call(bf16[512,256]{1,0:T(8,128)(2,1)S(1)} %get-tuple-element.9.a, f32[128,256]{1,0:T(8,128)S(1)} %get-tuple-element.10.b, f32[1,256]{1,0:T(1,128)S(1)} %get-tuple-element.11.c), custom_call_target="tpu_custom_call" | custom-call | tf_op jit(solution)/shard_map/pallas_call | solution.py:397
